TPU v7x, 768 devices: a whole 4x8x12 slice. The times are simulated.
768 devices in a mesh: dp: 12 (over z_lo, core), node: 64 (over y, x, z_hi).
Axes of the slice: x: 4, y: 8, z: 12 (z_hi: 2, z_lo: 6; z = z_hi * 6 + z_lo), core: 2. Of those that a mesh axis runs over, the one named last changes fastest.
Arguments:
- tokens: bfloat16 [24, 256, 8192], P('dp'), may hold values from -9 to 9, as said below
- context_gradient: bfloat16 [24, 256, 8192], P('dp', None, 'node'), may hold values from -6 to 6
- query_codes: bfloat16 [72, 128, 8192], P('dp', None, 'node'), may hold values from -1 to 1
- query_scale: bfloat16 [72, 8192], P('dp', 'node'), may hold values from 0.009887695 to 0.03857422
- keyval_codes: bfloat16 [72, 128, 2048], P('dp', None, 'node'), may hold values from -1 to 1
- keyval_scale: bfloat16 [72, 2048], P('dp', 'node'), may hold values from 0.009887695 to 0.03857422
Outputs:
- context: bfloat16 [24, 256, 8192], P('dp', None, 'node')
- grad_query: float32 [72, 128, 8192], P('dp', None, 'node')
- grad_keyval: float32 [72, 128, 2048], P('dp', None, 'node')
Inputs may be any that keep to these rules, and one draw needn't show every extreme that they name: `tokens`: activations of the layer's input.
All inputs are finite; a program needn't handle non-finite values.
Results may differ from a plain program's by a relative error of at most 0.02.
The roundings to bfloat16 on the way count: a program that leaves them out, or rounds other values in their place, can miss the bound.
Values may be sent and summed in bfloat16 or wider, within the bound.
A program may use at most 32 MiB of HBM per device.

v0:
```python
import math

import jax
import jax.numpy as jnp
from jax import lax
from jax.sharding import PartitionSpec as P

D = 8192
GROUP = 8
BLOCK = 128


def swapped(block, axis, distance):
    count = lax.axis_size(axis)
    route = []
    for low in range(count):
        high = low | 1 << distance
        if high != low and high < count:
            route += [(low, high), (high, low)]
    return lax.ppermute(block, axis, route)


def dequantize(code_block, scales):
    joined = code_block.astype(jnp.float32) * scales.astype(jnp.float32)[:, None, :]
    return joined.astype(jnp.bfloat16).reshape(-1, code_block.shape[2])


def per_device(tokens, context_gradient, query_codes, query_scale, keyval_codes, keyval_scale):
    seq_count, length, width_model = tokens.shape
    tok_count = seq_count * length
    tok_rows = tokens.reshape(tok_count, width_model)
    head_dim = query_codes.shape[2]
    keyval_width = keyval_codes.shape[2]
    shard_rows = query_codes.shape[0] * BLOCK
    padded = jnp.pad(tok_rows, ((0, 0), (0, shard_rows * lax.axis_size("dp") - D)))
    gathered = (
        lax.all_gather(query_codes, "dp", axis=0, tiled=True),
        lax.all_gather(query_scale, "dp", axis=0, tiled=True),
        lax.all_gather(keyval_codes, "dp", axis=0, tiled=True),
        lax.all_gather(keyval_scale, "dp", axis=0, tiled=True),
    )
    block_list = D // BLOCK
    w_query = dequantize(gathered[0][:block_list], gathered[1][:block_list])
    w_keyval = dequantize(gathered[2][:block_list], gathered[3][:block_list])
    queries = jnp.dot(tok_rows, w_query, preferred_element_type=jnp.float32)
    keyval = jnp.dot(tok_rows, w_keyval, preferred_element_type=jnp.float32)
    queries = queries.astype(jnp.bfloat16)
    keyval = keyval.astype(jnp.bfloat16)
    member = lax.axis_index("node") % GROUP
    section_count = GROUP.bit_length() - 1
    group_block = keyval
    for section_bit in range(section_count):
        partner = swapped(group_block, "node", section_bit)
        side_bit = member // 2**section_bit % 2
        group_block = jnp.where(
            side_bit == 1,
            jnp.concatenate([partner, group_block], axis=1),
            jnp.concatenate([group_block, partner], axis=1),
        )
    own_block = group_block.reshape(tok_count, GROUP, 2, keyval_width // 2)
    key_matrix_rows = own_block[:, :, 0, :].reshape(seq_count, length, head_dim)
    value_matrix_rows = own_block[:, :, 1, :].reshape(seq_count, length, head_dim)
    query_matrix_rows = queries.reshape(seq_count, length, head_dim)
    factor = 1.0 / math.sqrt(head_dim)
    causal = lax.iota(jnp.int32, length)[:, None] >= lax.iota(jnp.int32, length)[None, :]
    scores = (
        jnp.einsum(
            "ivc,iqc->ivq", query_matrix_rows, key_matrix_rows, preferred_element_type=jnp.float32
        )
        * factor
    )
    scores = jnp.where(causal, scores, -jnp.inf)
    shifted = jnp.exp(scores - jnp.max(scores, axis=-1, keepdims=True))
    attend = shifted / jnp.sum(shifted, axis=-1, keepdims=True)
    attend_lower_half = attend.astype(jnp.bfloat16)
    context = jnp.einsum(
        "tcz,tzf->tcf", attend_lower_half, value_matrix_rows, preferred_element_type=jnp.float32
    ).astype(jnp.bfloat16)
    back_attend = jnp.einsum(
        "ivc,iqc->ivq", context_gradient, value_matrix_rows, preferred_element_type=jnp.float32
    )
    center = jnp.sum(back_attend * attend, axis=-1, keepdims=True)
    scores_backward = (attend * (back_attend - center) * factor).astype(jnp.bfloat16)
    back_query = jnp.einsum(
        "tcz,tzf->tcf", scores_backward, key_matrix_rows, preferred_element_type=jnp.float32
    )
    back_query = back_query.astype(jnp.bfloat16).reshape(tok_count, head_dim)
    back_key = jnp.einsum(
        "foz,fok->fzk", scores_backward, query_matrix_rows, preferred_element_type=jnp.float32
    )
    back_value = jnp.einsum(
        "foz,fok->fzk", attend_lower_half, context_gradient, preferred_element_type=jnp.float32
    )
    own_term = jnp.stack(
        [
            back_key.reshape(tok_count, GROUP, keyval_width // 2),
            back_value.reshape(tok_count, GROUP, keyval_width // 2),
        ],
        axis=2,
    )
    own_term = own_term.reshape(tok_count, GROUP, keyval_width)
    current = own_term
    for section_bit in reversed(range(section_count)):
        half_count = current.shape[1] // 2
        low_half = current[:, :half_count]
        high_half = current[:, half_count:]
        side_bit = member // 2**section_bit % 2
        kept_half = jnp.where(side_bit == 1, high_half, low_half)
        sent_half = jnp.where(side_bit == 1, low_half, high_half)
        current = kept_half + swapped(sent_half, "node", section_bit)
    back_keyval = current.reshape(tok_count, keyval_width)
    back_keyval = back_keyval.astype(jnp.bfloat16)
    back_joined = jnp.concatenate([back_query, back_keyval], axis=1)
    partial_value = lax.dot_general(
        padded, back_joined, (((0,), (0,)), ((), ())), preferred_element_type=jnp.float32
    )
    summed = lax.psum_scatter(
        lax.optimization_barrier(partial_value.astype(jnp.bfloat16))
        .astype(jnp.float32)
        .astype(jnp.bfloat16),
        "dp",
        scatter_dimension=0,
        tiled=True,
    ).astype(jnp.float32)
    grad_query = summed[:, :head_dim].reshape(query_codes.shape)
    grad_keyval = summed[:, head_dim:].reshape(keyval_codes.shape)
    return (context, grad_query, grad_keyval)


def solution(mesh):
    return jax.shard_map(
        per_device,
        mesh=mesh,
        in_specs=(
            P("dp", None, None),
            P("dp", None, "node"),
            P("dp", None, "node"),
            P("dp", "node"),
            P("dp", None, "node"),
            P("dp", "node"),
        ),
        out_specs=(P("dp", None, "node"), P("dp", None, "node"), P("dp", None, "node")),
        check_vma=False,
    )
```

profile of v0, /device:TPU:6, one launch (start us, length us, event | category | flops | bytes accessed | tf_op | source)
XLA Modules:
  0.0 239.1 jit_solution(15362159736425387402)
XLA Ops:
  7.2 0.7 all-gather.4.cloned.1.call-update
  8.0 24.1 %all-gather.1 = bf16[12,6,32]{2,1,0:T(8,128)(2,1)S(1)} all-gather(bf16[1,6,32]{2,1,0:T(8,128)(2,1)} %bitcast.82), channel_id=1, replica_groups=mesh['dp'=12,'node'=64] {'dp'}, dimensions={0}, use_global_device_ids=true | all-gather | bytes 4992 | tf_op jit(solution)/shard_map/all_gather | solution.py:40
  32.1 26.0 %all_gather.14 = bf16[72,128,32]{1,2,0:T(8,128)(2,1)S(1)} all-gather(bf16[6,128,32]{1,2,0:T(8,128)(2,1)} %param.10), channel_id=1, replica_groups=mesh['dp'=12,'node'=64] {'dp'}, dimensions={0}, use_global_device_ids=true | all-gather | bytes 638976 | tf_op jit(solution)/shard_map/all_gather | solution.py:39
  58.1 6.1 %convolution_convert_fusion.4 = bf16[32,512]{1,0:T(8,128)(2,1)S(1)} fusion(bf16[512,8192]{1,0:T(8,128)(2,1)} %bitcast.65, bf16[72,128,32]{1,2,0:T(8,128)(2,1)S(1)} %all_gather.14, f32[64,32]{1,0:T(8,128)S(1)} %slice_convert_fusion), kind=kOutput, calls=%fused_computation.18 | convolution fusion | flops 269238272 | bytes 8978432 | tf_op jit(solution)/shard_map/dot_general | solution.py:46
  64.2 8.6 %collective-permute-start = (bf16[512,32]{0,1:T(8,128)(2,1)S(1)}, bf16[512,32]{0,1:T(8,128)(2,1)S(1)}, u32[]{:S(2)}, u32[]{:S(2)}) collective-permute-start(bf16[512,32]{0,1:T(8,128)(2,1)S(1)} %bitcast.72), channel_id=1, source_target_pairs={{0,1},{1,0},{2,3},{3,2},{4,5},{5,4},{6,7},{7,6},{8,9},{9,8},{10,11... | collective-permute-start | bytes 98312 | tf_op jit(solution)/shard_map/ppermute | solution.py:20
  72.9 19.8 %all-gather = bf16[12,6,128]{2,1,0:T(8,128)(2,1)S(1)} all-gather(bf16[1,6,128]{2,1,0:T(8,128)(2,1)S(1)} %bitcast.83), channel_id=1, replica_groups=mesh['dp'=12,'node'=64] {'dp'}, dimensions={0}, use_global_device_ids=true | all-gather | bytes 19968 | tf_op jit(solution)/shard_map/all_gather | solution.py:38
  92.9 2.8 %collective-permute-start.1 = (bf16[512,64]{0,1:T(8,128)(2,1)S(1)}, bf16[512,64]{0,1:T(8,128)(2,1)S(1)}, u32[]{:S(2)}, u32[]{:S(2)}) collective-permute-start(bf16[512,64]{0,1:T(8,128)(2,1)S(1)} %maximum_select_fusion.3), channel_id=1, source_target_pairs={{0,2},{2,0},{1,3},{3,1},{4,6},{6,4},{5,7},{7,5},{8,10},{10,8},{9,1... | collective-permute-start | bytes 196616 | tf_op jit(solution)/shard_map/ppermute | solution.py:20
  95.8 3.4 %collective-permute-done.1 = bf16[512,64]{0,1:T(8,128)(2,1)S(1)} collective-permute-done((bf16[512,64]{0,1:T(8,128)(2,1)S(1)}, bf16[512,64]{0,1:T(8,128)(2,1)S(1)}, u32[]{:S(2)}, u32[]{:S(2)}) %collective-permute-start.1) | collective-permute-done | bytes 65568 | tf_op jit(solution)/shard_map/ppermute | solution.py:20
  99.2 3.4 %collective-permute-start.2 = (bf16[512,128]{0,1:T(8,128)(2,1)S(1)}, bf16[512,128]{0,1:T(8,128)(2,1)S(1)}, u32[]{:S(2)}, u32[]{:S(2)}) collective-permute-start(bf16[512,128]{0,1:T(8,128)(2,1)S(1)} %maximum_select_fusion.1), channel_id=1, source_target_pairs={{0,4},{4,0},{1,5},{5,1},{2,6},{6,2},{3,7},{7,3},{8,12},{12,8},{9,1... | collective-permute-start | bytes 393224 | tf_op jit(solution)/shard_map/ppermute | solution.py:20
  102.6 4.9 %collective-permute-done.2 = bf16[512,128]{0,1:T(8,128)(2,1)S(1)} collective-permute-done((bf16[512,128]{0,1:T(8,128)(2,1)S(1)}, bf16[512,128]{0,1:T(8,128)(2,1)S(1)}, u32[]{:S(2)}, u32[]{:S(2)}) %collective-permute-start.2) | collective-permute-done | bytes 131104 | tf_op jit(solution)/shard_map/ppermute | solution.py:20
  108.2 2.2 multiply_convert_fusion
  110.5 6.3 %fusion.10 = bf16[512,128]{0,1:T(8,128)(2,1)S(1)} fusion(bf16[8192,128]{1,0:T(8,128)(2,1)S(1)} %bitcast.68, bf16[512,8192]{1,0:T(8,128)(2,1)} %bitcast.66), kind=kOutput, calls=%fused_computation.17 | convolution fusion | flops 1073807360 | bytes 10616832 | tf_op jit(solution)/shard_map/dot_general | solution.py:45
  118.9 3.4 %collective-permute-start.3 = (f32[512,4,32]{0,2,1:T(8,128)S(1)}, f32[512,4,32]{0,2,1:T(8,128)S(1)}, u32[]{:S(2)}, u32[]{:S(2)}) collective-permute-start(f32[512,4,32]{0,2,1:T(8,128)S(1)} %slice_select_fusion), channel_id=1, source_target_pairs={{0,4},{4,0},{1,5},{5,1},{2,6},{6,2},{3,7},{7,3},{8,12},{12,8},{9,1... | collective-permute-start | bytes 786440 | tf_op jit(solution)/shard_map/ppermute | solution.py:20
  122.4 6.5 %collective-permute-done.3 = f32[512,4,32]{0,2,1:T(8,128)S(1)} collective-permute-done((f32[512,4,32]{0,2,1:T(8,128)S(1)}, f32[512,4,32]{0,2,1:T(8,128)S(1)}, u32[]{:S(2)}, u32[]{:S(2)}) %collective-permute-start.3) | collective-permute-done | bytes 262176 | tf_op jit(solution)/shard_map/ppermute | solution.py:20
  129.0 2.8 %collective-permute-start.4 = (f32[512,2,32]{0,2,1:T(8,128)S(1)}, f32[512,2,32]{0,2,1:T(8,128)S(1)}, u32[]{:S(2)}, u32[]{:S(2)}) collective-permute-start(f32[512,2,32]{0,2,1:T(8,128)S(1)} %slice_select_fusion.1), channel_id=1, source_target_pairs={{0,2},{2,0},{1,3},{3,1},{4,6},{6,4},{5,7},{7,5},{8,10},{10,8},{9,1... | collective-permute-start | bytes 393224 | tf_op jit(solution)/shard_map/ppermute | solution.py:20
  131.9 4.0 %collective-permute-done.4 = f32[512,2,32]{0,2,1:T(8,128)S(1)} collective-permute-done((f32[512,2,32]{0,2,1:T(8,128)S(1)}, f32[512,2,32]{0,2,1:T(8,128)S(1)}, u32[]{:S(2)}, u32[]{:S(2)}) %collective-permute-start.4) | collective-permute-done | bytes 131104 | tf_op jit(solution)/shard_map/ppermute | solution.py:20
  135.9 5.4 %collective-permute-start.5 = (f32[512,1,32]{0,2,1:T(8,128)S(1)}, f32[512,1,32]{0,2,1:T(8,128)S(1)}, u32[]{:S(2)}, u32[]{:S(2)}) collective-permute-start(f32[512,1,32]{0,2,1:T(8,128)S(1)} %slice_select_fusion.2), channel_id=1, source_target_pairs={{0,1},{1,0},{2,3},{3,2},{4,5},{5,4},{6,7},{7,6},{8,9},{9,8},{10,11... | collective-permute-start | bytes 196616 | tf_op jit(solution)/shard_map/ppermute | solution.py:20
  141.7 6.7 %collective-permute-done.5 = f32[512,1,32]{0,2,1:T(8,128)S(1)} collective-permute-done((f32[512,1,32]{0,2,1:T(8,128)S(1)}, f32[512,1,32]{0,2,1:T(8,128)S(1)}, u32[]{:S(2)}, u32[]{:S(2)}) %collective-permute-start.5) | collective-permute-done | bytes 65568 | tf_op jit(solution)/shard_map/ppermute | solution.py:20
  148.5 6.7 %convolution_convert_fusion = bf16[9216,160]{0,1:T(8,128)(2,1)} fusion(bf16[512,8192]{1,0:T(8,128)(2,1)} %bitcast.67, bf16[512,32]{1,0:T(8,128)(2,1)S(1)} %copy.61, bf16[512,128]{1,0:T(8,128)(2,1)S(1)} %bitcast.84), kind=kOutput, calls=%fused_computation.2 | convolution fusion | flops 1511751680 | bytes 11501568 | tf_op jit(solution)/shard_map/dot_general | solution.py:114
  155.3 1.2 convolution_convert_fusion.2
  156.5 72.3 %reduce-scatter.2.cloned.1.call-done = bf16[768,160]{0,1:T(8,128)(2,1)} async-done(((bf16[9216,160]{0,1:T(8,128)(2,1)}), bf16[768,160]{0,1:T(8,128)(2,1)}) %reduce-scatter.2.cloned.1.call-update) | async-done | bytes 245776 | tf_op jit(solution)/shard_map/reduce_scatter | solution.py:117
  228.8 1.0 slice.68
  229.7 0.9 copy.62
  230.7 1.0 convert_element_type.75
  (44 shorter events, 4.3 us)
Async XLA Ops:
  7.2 100.8 %copy-start = (bf16[2,256,128]{2,1,0:T(8,128)(2,1)S(1)}, bf16[2,256,128]{2,1,0:T(8,128)(2,1)}, u32[]{:S(2)}) copy-start(bf16[2,256,128]{2,1,0:T(8,128)(2,1)} %param.7) | copy-start | bytes 393220
  7.2 101.0 %all-gather.4.cloned.1.call-start = ((), (), s32[]{:S(2)}) async-start(), calls=%async_computation.1 | async-start | bytes 2555904 | tf_op jit(solution)/shard_map/all_gather | solution.py:37
  7.9 220.9 %reduce-scatter.2.cloned.1.call-start = ((), (), s32[]{:S(2)}) async-start(), calls=%async_computation.2 | async-start | bytes 3194880 | tf_op jit(solution)/shard_map/reduce_scatter | solution.py:117
  58.1 14.7 %copy-start.1 = (bf16[6,128]{1,0:T(8,128)(2,1)S(1)}, bf16[6,128]{1,0:T(8,128)(2,1)}, u32[]{:S(2)}) copy-start(bf16[6,128]{1,0:T(8,128)(2,1)} %param.9) | copy-start | bytes 4612
  64.2 28.7 %collective-permute-start = (bf16[512,32]{0,1:T(8,128)(2,1)S(1)}, bf16[512,32]{0,1:T(8,128)(2,1)S(1)}, u32[]{:S(2)}, u32[]{:S(2)}) collective-permute-start(bf16[512,32]{0,1:T(8,128)(2,1)S(1)} %bitcast.72), channel_id=1, source_target_pairs={{0,1},{1,0},{2,3},{3,2},{4,5},{5,4},{6,7},{7,6},{8,9},{9,8},{10,11... | collective-permute-start | bytes 98312 | tf_op jit(solution)/shard_map/ppermute | solution.py:20
  92.9 6.2 %collective-permute-start.1 = (bf16[512,64]{0,1:T(8,128)(2,1)S(1)}, bf16[512,64]{0,1:T(8,128)(2,1)S(1)}, u32[]{:S(2)}, u32[]{:S(2)}) collective-permute-start(bf16[512,64]{0,1:T(8,128)(2,1)S(1)} %maximum_select_fusion.3), channel_id=1, source_target_pairs={{0,2},{2,0},{1,3},{3,1},{4,6},{6,4},{5,7},{7,5},{8,10},{10,8},{9,1... | collective-permute-start | bytes 196616 | tf_op jit(solution)/shard_map/ppermute | solution.py:20
  99.2 8.4 %collective-permute-start.2 = (bf16[512,128]{0,1:T(8,128)(2,1)S(1)}, bf16[512,128]{0,1:T(8,128)(2,1)S(1)}, u32[]{:S(2)}, u32[]{:S(2)}) collective-permute-start(bf16[512,128]{0,1:T(8,128)(2,1)S(1)} %maximum_select_fusion.1), channel_id=1, source_target_pairs={{0,4},{4,0},{1,5},{5,1},{2,6},{6,2},{3,7},{7,3},{8,12},{12,8},{9,1... | collective-permute-start | bytes 393224 | tf_op jit(solution)/shard_map/ppermute | solution.py:20
  118.9 10.0 %collective-permute-start.3 = (f32[512,4,32]{0,2,1:T(8,128)S(1)}, f32[512,4,32]{0,2,1:T(8,128)S(1)}, u32[]{:S(2)}, u32[]{:S(2)}) collective-permute-start(f32[512,4,32]{0,2,1:T(8,128)S(1)} %slice_select_fusion), channel_id=1, source_target_pairs={{0,4},{4,0},{1,5},{5,1},{2,6},{6,2},{3,7},{7,3},{8,12},{12,8},{9,1... | collective-permute-start | bytes 786440 | tf_op jit(solution)/shard_map/ppermute | solution.py:20
  129.0 6.9 %collective-permute-start.4 = (f32[512,2,32]{0,2,1:T(8,128)S(1)}, f32[512,2,32]{0,2,1:T(8,128)S(1)}, u32[]{:S(2)}, u32[]{:S(2)}) collective-permute-start(f32[512,2,32]{0,2,1:T(8,128)S(1)} %slice_select_fusion.1), channel_id=1, source_target_pairs={{0,2},{2,0},{1,3},{3,1},{4,6},{6,4},{5,7},{7,5},{8,10},{10,8},{9,1... | collective-permute-start | bytes 393224 | tf_op jit(solution)/shard_map/ppermute | solution.py:20
  135.9 12.5 %collective-permute-start.5 = (f32[512,1,32]{0,2,1:T(8,128)S(1)}, f32[512,1,32]{0,2,1:T(8,128)S(1)}, u32[]{:S(2)}, u32[]{:S(2)}) collective-permute-start(f32[512,1,32]{0,2,1:T(8,128)S(1)} %slice_select_fusion.2), channel_id=1, source_target_pairs={{0,1},{1,0},{2,3},{3,2},{4,5},{5,4},{6,7},{7,6},{8,9},{9,8},{10,11... | collective-permute-start | bytes 196616 | tf_op jit(solution)/shard_map/ppermute | solution.py:20
Sparse Core Ops, SparseCore 0:
  10.4 81.4 all-gather.3
  155.4 73.3 reduce-scatter.1
where the time goes:
time: 240 us; the launch traced here: 239 us
  waiting for transfers between devices  98.5 us (41%)
  blocking collectives  70 us (29%)
  starting transfers between devices  26.7 us (11%)
  matrix products  22 us (9%)
  between operations  14.4 us (6%)
  local copies, waits for them, and re-layouts  3.93 us (2%)
  other arithmetic  3.56 us (1%)
    reduce_scatter x1, waiting for transfers between devices, per_device(): lax.psum_scatter(lax.optimization_barrier(partial_value.astype(jnp.bfloat...  72.3 us
    ppermute x6, starting transfers between devices, swapped(): return lax.ppermute(block, axis, route)  26.6 us
    all_gather x1, blocking collectives, per_device(): lax.all_gather(keyval_codes, 'dp', axis=0, tiled=True)  26 us
    ppermute x6, waiting for transfers between devices, swapped(): return lax.ppermute(block, axis, route)  25.5 us
    all_gather x1, blocking collectives, per_device(): lax.all_gather(keyval_scale, 'dp', axis=0, tiled=True)  24.1 us
    all_gather x1, blocking collectives, per_device(): lax.all_gather(query_scale, 'dp', axis=0, tiled=True)  19.8 us
    dot_general x1, matrix products, per_device(): lax.dot_general(padded, back_joined, (((0,), (0,)), ((), ())), preferred_...  6.72 us
    dot_general x1, matrix products, per_device(): queries = jnp.dot(tok_rows, w_query, preferred_element_type=jnp.float32)  6.29 us
  transfers between devices with their start and end apart: 8, of which 6 were waited for; matrix products, arithmetic and copies ran while one was open for 4% of the time, Pallas kernels for 0%

commit v1 on v0

v1 whole, which is shorter than its diff:
```python
import functools
import math

import jax
import jax.numpy as jnp
from jax import lax
from jax.experimental import pallas as pl
from jax.experimental.pallas import tpu as pltpu
from jax.sharding import PartitionSpec as P

MESH = pl.DeviceIdType.MESH
F32 = jnp.float32
BF16 = jnp.bfloat16
CHIPS = 6
LAST = CHIPS - 1
PIECES = 3
STEP = 256
GROUP = 8


def dot(a, b, dim_a=1, dim_b=0):
    return lax.dot_general(a, b, (((dim_a,), (dim_b,)), ((), ())), preferred_element_type=F32)


def kernel(
    tok_hbm, grad_ref, qc_ref, qs_ref, kc_ref, ks_ref,
    ctx_ref, gq_ref, gkv_ref,
    x_all, wq, wkv, kv, q_acc, kv_acc, back, kv_part, kv_low, kv_in, pair_sum, z_out, z_in,
    own_part, sib_out, sib_in, run_out, run_in,
    x_sem, ag_r, ag_s, rs_r, rs_s, sib_r, sib_s, kvz, kvx_s, kvx_r, dkz, dkx_s, dkx_r,
):
    dp = lax.axis_index("dp")
    node = lax.axis_index("node")
    chip = dp // 2
    core = dp % 2
    member = node % GROUP
    z_hi = member % 2
    x_at = member // 2
    sibling = {"dp": 2 * chip + 1 - core}
    z_twin = {"node": node + 1 - 2 * z_hi}
    tok_count = grad_ref.shape[0]
    length = 256

    def x_mate(delta):
        return {"node": node - member + ((x_at + delta) % 4) * 2 + z_hi}

    def place(way):
        return chip if way == 0 else LAST - chip

    def ahead(way):
        return {"dp": dp + 2 if way == 0 else dp - 2}

    def chip_of(way, position):
        return position if way == 0 else LAST - position

    def remote(src, dst, s_sem, r_sem, to):
        return pltpu.make_async_remote_copy(
            src_ref=src, dst_ref=dst, send_sem=s_sem, recv_sem=r_sem, device_id=to, device_id_type=MESH
        )

    loaded = x_all.at[pl.ds(0, 32)]
    x_copy = pltpu.make_async_copy(loaded, loaded, x_sem)
    for i in range(32):
        pltpu.make_async_copy(tok_hbm.at[:, pl.ds(i * STEP, STEP)], x_all.at[i], x_sem).start()
    x_all[32:36] = jnp.zeros((4, tok_count, STEP), BF16)

    for b in range(6):
        rows = pl.ds(b * 128, 128)
        wq[dp, rows, :] = (qc_ref[b].astype(F32) * qs_ref[b : b + 1, :].astype(F32)).astype(BF16)
        wkv[dp, :, rows] = (kc_ref[b].astype(F32) * ks_ref[:, b : b + 1].astype(F32)).astype(BF16)

    barrier = pltpu.get_barrier_semaphore()
    for to in (sibling, z_twin, x_mate(1), x_mate(2), x_mate(3)):
        pl.semaphore_signal(barrier, inc=1, device_id=to, device_id_type=MESH)
    for way in range(2):
        @pl.when(place(way) < LAST)
        def _():
            pl.semaphore_signal(barrier, inc=1, device_id=ahead(way), device_id_type=MESH)
    pl.semaphore_wait(barrier, 7 - (chip == 0).astype(jnp.int32) - (chip == LAST).astype(jnp.int32))

    def chunk(owner, piece):
        if piece == 0:
            return wkv.at[owner]
        return wq.at[owner, pl.ds((piece - 1) * STEP, STEP), :]

    def ag_copy(src_chip, piece, to, s_sem):
        owner = 2 * src_chip + core
        part = chunk(owner, piece)
        return remote(part, part, s_sem, ag_r.at[owner, piece], to)

    def ag_wait(owner, piece):
        part = chunk(owner, piece)
        remote(part, part, ag_s.at[2, 0, piece], ag_r.at[owner, piece], sibling).wait_recv()

    def ag_send(src_chip, piece, only=(0, 1)):
        for way in only:
            @pl.when(place(way) < LAST)
            def _():
                ag_copy(src_chip, piece, ahead(way), ag_s.at[way, src_chip, piece]).start()
        ag_copy(src_chip, piece, sibling, ag_s.at[2, src_chip, piece]).start()

    def use_kv(owner):
        total = kv_acc[...]
        for p in range(PIECES):
            total += dot(wkv[owner, :, p * STEP : (p + 1) * STEP], x_all[owner * PIECES + p], 1, 1)
        kv_acc[...] = total

    def use_q(owner, p):
        q_acc[...] += dot(x_all[owner * PIECES + p], wq[owner, p * STEP : (p + 1) * STEP, :])

    def each_source(distance, body):
        for way in range(2):
            src = chip_of(way, place(way) - distance)
            @pl.when(place(way) >= distance)
            def _():
                body(way, src)

    def take(src, piece):
        other = 2 * src + 1 - core
        ag_wait(other, piece)
        if piece == 0:
            use_kv(2 * src + core)
            use_kv(other)
        else:
            use_q(2 * src + core, piece - 1)
            use_q(other, piece - 1)

    q_acc[...] = jnp.zeros_like(q_acc)
    kv_acc[...] = jnp.zeros_like(kv_acc)
    ag_send(chip, 0)
    ag_send(chip, 1)
    x_copy.wait()

    def pass_on(distance, piece):
        def body(way, src):
            ag_wait(2 * src + core, piece)
            ag_send(src, piece, (way,))
        each_source(distance, body)

    pass_on(1, 0)
    ag_send(chip, 2)
    take(chip, 0)
    pass_on(2, 0)
    ag_send(chip, 3)
    each_source(1, lambda way, src: take(src, 0))

    def kv_step(d, carry):
        pass_on(d, 0)
        each_source(d - 1, lambda way, src: take(src, 0))
        return carry

    lax.fori_loop(3, CHIPS, kv_step, 0)
    each_source(LAST, lambda way, src: take(src, 0))
    kv[member] = kv_acc[...].astype(BF16).reshape(2, 16, tok_count)
    z_copy = remote(kv.at[member], kv.at[member], kvz.at[0], kvz.at[1], z_twin)
    z_copy.start()

    def q_step(d, carry):
        for p in range(PIECES):
            pass_on(d, p + 1)

            @pl.when(d == 1)
            def _():
                take(chip, p + 1)

            @pl.when(d > 1)
            def _():
                each_source(d - 1, lambda way, src: take(src, p + 1))
        return carry

    lax.fori_loop(1, 2, q_step, 0)

    pair = pl.ds(x_at * 2, 2)
    z_copy.wait()
    kv_copies = []
    for delta in (1, 2, 3):
        copy = remote(kv.at[pair], kv.at[pair], kvx_s.at[delta - 1], kvx_r.at[delta - 1], x_mate(delta))
        copy.start()
        kv_copies.append(copy)

    lax.fori_loop(2, CHIPS, q_step, 0)
    for p in range(PIECES):
        each_source(LAST, lambda way, src: take(src, p + 1))
    for copy in kv_copies:
        copy.wait()

    factor = 1.0 / math.sqrt(128)
    keys = kv[:, 0].reshape(128, tok_count)
    values = kv[:, 1].reshape(128, tok_count)
    seen = lax.broadcasted_iota(jnp.int32, (length, length), 0) >= lax.broadcasted_iota(
        jnp.int32, (length, length), 1
    )
    for s in range(tok_count // length):
        at = slice(s * length, (s + 1) * length)
        queries = q_acc[at, :].astype(BF16)
        grad = grad_ref[at, :]
        key_t, value_t = keys[:, at], values[:, at]
        scores = jnp.where(seen, dot(queries, key_t) * factor, -jnp.inf)
        shifted = jnp.exp(scores - jnp.max(scores, axis=1, keepdims=True))
        attend = shifted / jnp.sum(shifted, axis=1, keepdims=True)
        low = attend.astype(BF16)
        back_attend = dot(grad, value_t)
        center = jnp.sum(back_attend * attend, axis=1, keepdims=True)
        back_scores = (attend * (back_attend - center) * factor).astype(BF16)
        kv_part[:, 0, :, at] = dot(queries, back_scores, 0, 0).reshape(GROUP, 16, length)
        kv_part[:, 1, :, at] = dot(grad, low, 0, 0).reshape(GROUP, 16, length)
        back[0:128, at] = dot(key_t, back_scores, 1, 1).astype(BF16)
        ctx_ref[at, :] = dot(low, value_t, 1, 1).astype(BF16)
    kv_low[...] = kv_part[...].astype(BF16)
    dk_copies = []
    for delta in (1, 2, 3):
        theirs = pl.ds(((x_at + delta) % 4) * 2, 2)
        copy = remote(kv_low.at[theirs], kv_in.at[delta - 1], dkx_s.at[delta - 1], dkx_r.at[delta - 1], x_mate(delta))
        copy.start()
        dk_copies.append(copy)

    def sib_copy(dest, piece):
        if piece < PIECES:
            src, dst = sib_out.at[dest, piece, pl.ds(0, 128)], sib_in.at[dest, piece, pl.ds(0, 128)]
        else:
            src, dst = sib_out.at[dest, :, pl.ds(128, 32)], sib_in.at[dest, :, pl.ds(128, 32)]
        return remote(src, dst, sib_s.at[dest, piece], sib_r.at[dest, piece], sibling)

    def run_copy(way, dest, piece):
        if piece < PIECES:
            src, dst = run_out.at[dest, piece, pl.ds(0, 128)], run_in.at[way, dest, piece, pl.ds(0, 128)]
        else:
            src, dst = run_out.at[dest, :, pl.ds(128, 32)], run_in.at[way, dest, :, pl.ds(128, 32)]
        return remote(src, dst, rs_s.at[dest, piece], rs_r.at[way, dest, piece], ahead(way))

    def terms(dest, rows, piece):
        theirs = (2 * dest + 1 - core) * PIECES
        ours = (2 * dest + core) * PIECES
        pieces = (piece,) if piece < PIECES else range(PIECES)
        for p in pieces:
            sib_out[dest, p, rows, :] = dot(back[rows, :], x_all[theirs + p]).astype(BF16)
        sib_copy(dest, piece).start()
        for p in pieces:
            own_part[dest, p, rows, :] = dot(back[rows, :], x_all[ours + p]).astype(BF16)

    q_rows, kv_rows = slice(0, 128), slice(128, 160)

    def q_terms(dest):
        for p in range(PIECES):
            terms(dest, q_rows, p)

    def each_dest(time, body):
        for way in range(2):
            dest = chip_of(way, LAST - time + place(way))
            @pl.when(time >= place(way))
            def _():
                body(way, dest)

    def combine(way, dest, piece):
        rows = q_rows if piece < PIECES else kv_rows
        pieces = (piece,) if piece < PIECES else range(PIECES)
        sib_copy(dest, piece).wait_recv()

        @pl.when(place(way) > 0)
        def _():
            run_copy(way, dest, piece).wait_recv()
            for p in pieces:
                run_out[dest, p, rows, :] = (
                    own_part[dest, p, rows, :].astype(F32)
                    + sib_in[dest, p, rows, :].astype(F32)
                    + run_in[way, dest, p, rows, :].astype(F32)
                ).astype(BF16)

        @pl.when(place(way) == 0)
        def _():
            for p in pieces:
                run_out[dest, p, rows, :] = (
                    own_part[dest, p, rows, :].astype(F32) + sib_in[dest, p, rows, :].astype(F32)
                ).astype(BF16)

        run_copy(way, dest, piece).start()

    def q_time(time, carry):
        @pl.when(time < LAST - 1)
        def _():
            each_dest(time + 1, lambda way, dest: q_terms(dest))

        for p in range(PIECES):
            each_dest(time, lambda way, dest: combine(way, dest, p))
        return carry

    each_dest(0, lambda way, dest: q_terms(dest))
    lax.fori_loop(0, 2, q_time, 0)

    for copy in dk_copies:
        copy.wait()
    pair_sum[...] = (
        kv_part[pair]
        + kv_in[0].astype(F32)
        + kv_in[1].astype(F32)
        + kv_in[2].astype(F32)
    )
    z_out[...] = pair_sum[1 - z_hi].astype(BF16)
    dz_copy = remote(z_out, z_in, dkz.at[0], dkz.at[1], z_twin)
    dz_copy.start()
    lax.fori_loop(2, 3, q_time, 0)
    dz_copy.wait()
    back[128:160, :] = (pair_sum[z_hi] + z_in[...].astype(F32)).astype(BF16).reshape(32, tok_count)

    def kv_terms(dest, carry):
        terms(dest, kv_rows, PIECES)
        return carry

    lax.fori_loop(0, CHIPS, kv_terms, 0)

    def kv_time(time, carry):
        each_dest(time, lambda way, dest: combine(way, dest, PIECES))
        return carry

    def both(time, carry):
        kv_time(time - 3, 0)
        return q_time(time, carry)

    lax.fori_loop(3, CHIPS - 1, both, 0)
    q_terms(chip)
    lax.fori_loop(2, CHIPS - 1, kv_time, 0)

    for piece in range(PIECES + 1):
        rows = q_rows if piece < PIECES else kv_rows
        pieces = (piece,) if piece < PIECES else range(PIECES)
        sib_copy(chip, piece).wait_recv()
        for p in pieces:
            run_sum = own_part[chip, p, rows, :].astype(F32) + sib_in[chip, p, rows, :].astype(F32)
            if piece < PIECES:
                gq_ref[2 * p : 2 * p + 2] = run_sum.T.reshape(2, 128, 128)
            else:
                gkv_ref[2 * p] = run_sum[:, 0:128]
                gkv_ref[2 * p + 1] = run_sum[:, 128:256]
        for way in range(2):
            @pl.when(place(way) > 0)
            def _():
                run_copy(way, chip, piece).wait_recv()
                for p in pieces:
                    more = run_in[way, chip, p, rows, :].astype(F32)
                    if piece < PIECES:
                        gq_ref[2 * p : 2 * p + 2] += more.T.reshape(2, 128, 128)
                    else:
                        gkv_ref[2 * p] += more[:, 0:128]
                        gkv_ref[2 * p + 1] += more[:, 128:256]

    def drain(at, carry):
        for piece in range(PIECES + 1):
            for way in range(2):
                @pl.when((place(way) < LAST) & ((at <= chip) if way == 0 else (at >= chip)))
                def _():
                    ag_copy(at, piece, sibling, ag_s.at[way, at, piece]).wait_send()

                @pl.when((at > chip) if way == 0 else (at < chip))
                def _():
                    run_copy(way, at, piece).wait_send()
            ag_copy(at, piece, sibling, ag_s.at[2, at, piece]).wait_send()
            sib_copy(at, piece).wait_send()
        return carry

    lax.fori_loop(0, CHIPS, drain, 0)


def per_device(tokens, context_gradient, query_codes, query_scale, keyval_codes, keyval_scale):
    seq_count, length, width = tokens.shape
    tok_count = seq_count * length
    dma = pltpu.SemaphoreType.DMA
    vmem = pl.BlockSpec(memory_space=pltpu.VMEM)
    out = pl.pallas_call(
        kernel,
        out_shape=(
            jax.ShapeDtypeStruct((tok_count, 128), BF16),
            jax.ShapeDtypeStruct((6, 128, 128), F32),
            jax.ShapeDtypeStruct((6, 32, 128), F32),
        ),
        in_specs=[pl.BlockSpec(memory_space=pl.ANY)] + [vmem] * 5,
        out_specs=(vmem, vmem, vmem),
        scratch_shapes=[
            pltpu.VMEM((36, tok_count, STEP), BF16),
            pltpu.VMEM((12, 768, 128), BF16),
            pltpu.VMEM((12, 32, 768), BF16),
            pltpu.VMEM((GROUP, 2, 16, tok_count), BF16),
            pltpu.VMEM((tok_count, 128), F32),
            pltpu.VMEM((32, tok_count), F32),
            pltpu.VMEM((160, tok_count), BF16),
            pltpu.VMEM((GROUP, 2, 16, tok_count), F32),
            pltpu.VMEM((GROUP, 2, 16, tok_count), BF16),
            pltpu.VMEM((3, 2, 2, 16, tok_count), BF16),
            pltpu.VMEM((2, 2, 16, tok_count), F32),
            pltpu.VMEM((2, 16, tok_count), BF16),
            pltpu.VMEM((2, 16, tok_count), BF16),
            pltpu.VMEM((CHIPS, PIECES, 160, STEP), BF16),
            pltpu.VMEM((CHIPS, PIECES, 160, STEP), BF16),
            pltpu.VMEM((CHIPS, PIECES, 160, STEP), BF16),
            pltpu.VMEM((CHIPS, PIECES, 160, STEP), BF16),
            pltpu.VMEM((2, CHIPS, PIECES, 160, STEP), BF16),
            dma(()),
            dma((12, PIECES + 1)),
            dma((3, CHIPS, PIECES + 1)),
            dma((2, CHIPS, PIECES + 1)),
            dma((CHIPS, PIECES + 1)),
            dma((CHIPS, PIECES + 1)),
            dma((CHIPS, PIECES + 1)),
            dma((2,)),
            dma((3,)),
            dma((3,)),
            dma((2,)),
            dma((3,)),
            dma((3,)),
        ],
        compiler_params=pltpu.CompilerParams(
            collective_id=0, has_side_effects=True, vmem_limit_bytes=48 * 1024 * 1024
        ),
    )(
        tokens.reshape(tok_count, width),
        context_gradient.reshape(tok_count, 128),
        query_codes,
        query_scale,
        keyval_codes.transpose(0, 2, 1),
        keyval_scale.T,
    )
    return out[0].reshape(context_gradient.shape), out[1], out[2].transpose(0, 2, 1)


def solution(mesh):
    return jax.shard_map(
        per_device,
        mesh=mesh,
        in_specs=(
            P("dp", None, None),
            P("dp", None, "node"),
            P("dp", None, "node"),
            P("dp", "node"),
            P("dp", None, "node"),
            P("dp", "node"),
        ),
        out_specs=(P("dp", None, "node"), P("dp", None, "node"), P("dp", None, "node")),
        check_vma=False,
    )
```

time: 240 us -> 105 us (0.44)
  the two profiles are of different devices: /device:TPU:6 before, /device:TPU:1 now
where the time goes in v1:
time: 105 us; the launch traced here: 104 us
  Pallas kernels  97.3 us (93%)
  local copies, waits for them, and re-layouts  6.13 us (6%)
    pallas_call x1, Pallas kernels, per_device(): pl.pallas_call(kernel, out_shape=(jax.ShapeDtypeStruct((tok_count, 128),...  97.3 us
    unnamed x12, local copies, waits for them, and re-layouts  6.13 us

profile of v1, /device:TPU:1, one launch (start us, length us, event | category | flops | bytes accessed | tf_op | source)
XLA Modules:
  0.0 104.0 jit_solution(7300488494232993561)
XLA Ops:
  0.6 0.8 copy.9
  1.4 0.0 copy-start
  1.4 0.9 copy-done
  2.3 0.0 copy-start.1
  2.3 0.9 copy-done.1
  3.2 0.0 copy-start.2
  3.2 0.8 copy-done.2
  4.0 0.0 copy-start.3
  4.0 0.7 copy-done.3
  4.7 97.3 %shard_map.85 = (bf16[512,128]{1,0:T(8,128)(2,1)S(1)}, f32[6,128,128]{2,1,0:T(8,128)S(1)}, f32[6,32,128]{2,1,0:T(8,128)S(1)}) custom-call(bf16[512,8192]{1,0:T(8,128)(2,1)} %bitcast.11, bf16[512,128]{1,0:T(8,128)(2,1)S(1)} %bitcast.6, bf16[6,128,128]{2,1,0:T(8,128)(2,1)S(1)} %copy-done, bf16[6,128]{1,0:T(8,128)(2,1)S(1)} %copy-done.3, ...), custom_call_target="tpu_custom_call" | custom-call | tf_op jit(solution)/shard_map/pallas_call | solution.py:368
  102.0 0.7 copy.13
  102.6 0.7 copy.14
  103.4 0.6 copy.15
Async XLA Ops:
  1.4 0.9 copy-start
  2.3 0.9 copy-start.1
  3.2 0.8 copy-start.2
  4.0 0.7 copy-start.3

commit v2 on v1

--- a/solution.py
+++ b/solution.py
@@ -16,6 +16,7 @@
 PIECES = 3
 STEP = 256
 GROUP = 8
+VLIM = 60
 
 
 def dot(a, b, dim_a=1, dim_b=0):
@@ -23,11 +24,11 @@
 
 
 def kernel(
-    tok_hbm, grad_ref, qc_ref, qs_ref, kc_ref, ks_ref,
+    tok_hbm, grad_hbm, qc_hbm, qs_hbm, kc_hbm, ks_hbm,
     ctx_ref, gq_ref, gkv_ref,
-    x_all, wq, wkv, kv, q_acc, kv_acc, back, kv_part, kv_low, kv_in, pair_sum, z_out, z_in,
-    own_part, sib_out, sib_in, run_out, run_in,
-    x_sem, ag_r, ag_s, rs_r, rs_s, sib_r, sib_s, kvz, kvx_s, kvx_r, dkz, dkx_s, dkx_r,
+    grad_ref, qc_ref, qs_ref, kc_ref, ks_ref, x_all, wq, wkv, kv, q_acc, kv_acc, back, kv_part, kv_low, kv_in, pair_sum, z_out, z_in,
+    grad_values, q_low, attend_low, scores_low, own_part, sib_out, sib_in, run_out, run_in,
+    in_sem, x_sem, ag_r, ag_s, rs_r, rs_s, sib_r, sib_s, kvz, kvx_s, kvx_r, dkz, dkx_s, dkx_r,
 ):
     dp = lax.axis_index("dp")
     node = lax.axis_index("node")
@@ -39,7 +40,7 @@
     sibling = {"dp": 2 * chip + 1 - core}
     z_twin = {"node": node + 1 - 2 * z_hi}
     tok_count = grad_ref.shape[0]
-    length = 256
+    length = scores_low.shape[1]
 
     def x_mate(delta):
         return {"node": node - member + ((x_at + delta) % 4) * 2 + z_hi}
@@ -58,16 +59,18 @@
             src_ref=src, dst_ref=dst, send_sem=s_sem, recv_sem=r_sem, device_id=to, device_id_type=MESH
         )
 
+    small = [
+        pltpu.make_async_copy(src, dst, in_sem.at[i])
+        for i, (src, dst) in enumerate(
+            ((kc_hbm, kc_ref), (ks_hbm, ks_ref), (qc_hbm, qc_ref), (qs_hbm, qs_ref), (grad_hbm, grad_ref))
+        )
+    ]
+    for copy in small:
+        copy.start()
     loaded = x_all.at[pl.ds(0, 32)]
     x_copy = pltpu.make_async_copy(loaded, loaded, x_sem)
     for i in range(32):
         pltpu.make_async_copy(tok_hbm.at[:, pl.ds(i * STEP, STEP)], x_all.at[i], x_sem).start()
-    x_all[32:36] = jnp.zeros((4, tok_count, STEP), BF16)
-
-    for b in range(6):
-        rows = pl.ds(b * 128, 128)
-        wq[dp, rows, :] = (qc_ref[b].astype(F32) * qs_ref[b : b + 1, :].astype(F32)).astype(BF16)
-        wkv[dp, :, rows] = (kc_ref[b].astype(F32) * ks_ref[:, b : b + 1].astype(F32)).astype(BF16)
 
     barrier = pltpu.get_barrier_semaphore()
     for to in (sibling, z_twin, x_mate(1), x_mate(2), x_mate(3)):
@@ -76,12 +79,23 @@
         @pl.when(place(way) < LAST)
         def _():
             pl.semaphore_signal(barrier, inc=1, device_id=ahead(way), device_id_type=MESH)
+
+    for copy in small:
+        copy.wait()
+    diagonal = lax.broadcasted_iota(jnp.int32, (32, 32), 0) == lax.broadcasted_iota(jnp.int32, (32, 32), 1)
+    for b in range(6):
+        rows = pl.ds(b * 128, 128)
+        scale = jnp.where(diagonal, ks_ref[b : b + 1, :].astype(F32), 0.0).sum(axis=1, keepdims=True)
+        wkv[dp, :, rows] = (kc_ref[b].astype(F32) * scale).astype(BF16)
+    for b in range(6):
+        rows = pl.ds(b * 128, 128)
+        wq[dp, rows, :] = (qc_ref[b].astype(F32) * qs_ref[b : b + 1, :].astype(F32)).astype(BF16)
     pl.semaphore_wait(barrier, 7 - (chip == 0).astype(jnp.int32) - (chip == LAST).astype(jnp.int32))
 
     def chunk(owner, piece):
-        if piece == 0:
+        if isinstance(piece, int) and piece == 0:
             return wkv.at[owner]
-        return wq.at[owner, pl.ds((piece - 1) * STEP, STEP), :]
+        return wq.at[owner, pl.ds(pl.multiple_of((piece - 1) * STEP, STEP), STEP), :]
 
     def ag_copy(src_chip, piece, to, s_sem):
         owner = 2 * src_chip + core
@@ -105,8 +119,10 @@
             total += dot(wkv[owner, :, p * STEP : (p + 1) * STEP], x_all[owner * PIECES + p], 1, 1)
         kv_acc[...] = total
 
-    def use_q(owner, p):
-        q_acc[...] += dot(x_all[owner * PIECES + p], wq[owner, p * STEP : (p + 1) * STEP, :])
+    def use_q(owner, other, p):
+        q_acc[...] += dot(x_all[owner * PIECES + p], wq[owner, p * STEP : (p + 1) * STEP, :]) + dot(
+            x_all[other * PIECES + p], wq[other, p * STEP : (p + 1) * STEP, :]
+        )
 
     def each_source(distance, body):
         for way in range(2):
@@ -122,53 +138,51 @@
             use_kv(2 * src + core)
             use_kv(other)
         else:
-            use_q(2 * src + core, piece - 1)
-            use_q(other, piece - 1)
+            use_q(2 * src + core, other, piece - 1)
 
     q_acc[...] = jnp.zeros_like(q_acc)
     kv_acc[...] = jnp.zeros_like(kv_acc)
-    ag_send(chip, 0)
-    ag_send(chip, 1)
-    x_copy.wait()
-
     def pass_on(distance, piece):
         def body(way, src):
             ag_wait(2 * src + core, piece)
             ag_send(src, piece, (way,))
         each_source(distance, body)
 
+    ag_send(chip, 0)
+    ag_send(chip, 1)
     pass_on(1, 0)
     ag_send(chip, 2)
-    take(chip, 0)
     pass_on(2, 0)
     ag_send(chip, 3)
-    each_source(1, lambda way, src: take(src, 0))
+    x_all[32:36] = jnp.zeros((4, tok_count, STEP), BF16)
+    x_copy.wait()
+    take(chip, 0)
 
     def kv_step(d, carry):
         pass_on(d, 0)
-        each_source(d - 1, lambda way, src: take(src, 0))
+        pass_on(1, d - 2)
+        each_source(d - 2, lambda way, src: take(src, 0))
         return carry
 
     lax.fori_loop(3, CHIPS, kv_step, 0)
+    pass_on(2, 1)
+    each_source(LAST - 1, lambda way, src: take(src, 0))
     each_source(LAST, lambda way, src: take(src, 0))
     kv[member] = kv_acc[...].astype(BF16).reshape(2, 16, tok_count)
     z_copy = remote(kv.at[member], kv.at[member], kvz.at[0], kvz.at[1], z_twin)
     z_copy.start()
+    pass_on(2, 2)
+    pass_on(2, 3)
+    for p in range(PIECES):
+        take(chip, p + 1)
 
     def q_step(d, carry):
         for p in range(PIECES):
             pass_on(d, p + 1)
-
-            @pl.when(d == 1)
-            def _():
-                take(chip, p + 1)
-
-            @pl.when(d > 1)
-            def _():
-                each_source(d - 1, lambda way, src: take(src, p + 1))
+            each_source(d - 2, lambda way, src: take(src, p + 1))
         return carry
 
-    lax.fori_loop(1, 2, q_step, 0)
+    lax.fori_loop(3, 4, q_step, 0)
 
     pair = pl.ds(x_at * 2, 2)
     z_copy.wait()
@@ -178,11 +192,16 @@
         copy.start()
         kv_copies.append(copy)
 
-    lax.fori_loop(2, CHIPS, q_step, 0)
+    lax.fori_loop(4, CHIPS, q_step, 0)
+    for p in range(PIECES):
+        each_source(LAST - 1, lambda way, src: take(src, p + 1))
+    for copy in kv_copies:
+        copy.wait()
+    for s in range(tok_count // length):
+        at = slice(s * length, (s + 1) * length)
+        grad_values[at, :] = dot(grad_ref[at, :], kv[:, 1, :, at].reshape(128, length))
     for p in range(PIECES):
         each_source(LAST, lambda way, src: take(src, p + 1))
-    for copy in kv_copies:
-        copy.wait()
 
     factor = 1.0 / math.sqrt(128)
     keys = kv[:, 0].reshape(128, tok_count)
@@ -193,26 +212,35 @@
     for s in range(tok_count // length):
         at = slice(s * length, (s + 1) * length)
         queries = q_acc[at, :].astype(BF16)
-        grad = grad_ref[at, :]
-        key_t, value_t = keys[:, at], values[:, at]
-        scores = jnp.where(seen, dot(queries, key_t) * factor, -jnp.inf)
+        q_low[at, :] = queries
+        scores = jnp.where(seen, dot(queries, keys[:, at]) * factor, -jnp.inf)
         shifted = jnp.exp(scores - jnp.max(scores, axis=1, keepdims=True))
         attend = shifted / jnp.sum(shifted, axis=1, keepdims=True)
-        low = attend.astype(BF16)
-        back_attend = dot(grad, value_t)
+        attend_low[at, :] = attend.astype(BF16)
+        back_attend = grad_values[at, :]
         center = jnp.sum(back_attend * attend, axis=1, keepdims=True)
         back_scores = (attend * (back_attend - center) * factor).astype(BF16)
-        kv_part[:, 0, :, at] = dot(queries, back_scores, 0, 0).reshape(GROUP, 16, length)
-        kv_part[:, 1, :, at] = dot(grad, low, 0, 0).reshape(GROUP, 16, length)
-        back[0:128, at] = dot(key_t, back_scores, 1, 1).astype(BF16)
-        ctx_ref[at, :] = dot(low, value_t, 1, 1).astype(BF16)
-    kv_low[...] = kv_part[...].astype(BF16)
+        scores_low[at, :] = back_scores
+        back[0:128, at] = dot(keys[:, at], back_scores, 1, 1).astype(BF16)
+
+    def rest_of_attention():
+        for s in range(tok_count // length):
+            at = slice(s * length, (s + 1) * length)
+            kv_part[:, 0, :, at] = dot(q_low[at, :], scores_low[at, :], 0, 0).reshape(GROUP, 16, length)
+            kv_part[:, 1, :, at] = dot(grad_ref[at, :], attend_low[at, :], 0, 0).reshape(GROUP, 16, length)
+        kv_low[...] = kv_part[...].astype(BF16)
+        for copy in dk_copies:
+            copy.start()
+        for s in range(tok_count // length):
+            at = slice(s * length, (s + 1) * length)
+            ctx_ref[at, :] = dot(attend_low[at, :], values[:, at], 1, 1).astype(BF16)
+
     dk_copies = []
     for delta in (1, 2, 3):
         theirs = pl.ds(((x_at + delta) % 4) * 2, 2)
-        copy = remote(kv_low.at[theirs], kv_in.at[delta - 1], dkx_s.at[delta - 1], dkx_r.at[delta - 1], x_mate(delta))
-        copy.start()
-        dk_copies.append(copy)
+        dk_copies.append(
+            remote(kv_low.at[theirs], kv_in.at[delta - 1], dkx_s.at[delta - 1], dkx_r.at[delta - 1], x_mate(delta))
+        )
 
     def sib_copy(dest, piece):
         if piece < PIECES:
@@ -228,21 +256,20 @@
             src, dst = run_out.at[dest, :, pl.ds(128, 32)], run_in.at[way, dest, :, pl.ds(128, 32)]
         return remote(src, dst, rs_s.at[dest, piece], rs_r.at[way, dest, piece], ahead(way))
 
-    def terms(dest, rows, piece):
+    q_rows, kv_rows = slice(0, 128), slice(128, 160)
+
+    def terms(dest, rows):
         theirs = (2 * dest + 1 - core) * PIECES
         ours = (2 * dest + core) * PIECES
-        pieces = (piece,) if piece < PIECES else range(PIECES)
-        for p in pieces:
-            sib_out[dest, p, rows, :] = dot(back[rows, :], x_all[theirs + p]).astype(BF16)
-        sib_copy(dest, piece).start()
-        for p in pieces:
-            own_part[dest, p, rows, :] = dot(back[rows, :], x_all[ours + p]).astype(BF16)
-
-    q_rows, kv_rows = slice(0, 128), slice(128, 160)
-
-    def q_terms(dest):
+        low = back[rows, :]
+        sib = [dot(low, x_all[theirs + p]).astype(BF16) for p in range(PIECES)]
+        own = [dot(low, x_all[ours + p]).astype(BF16) for p in range(PIECES)]
         for p in range(PIECES):
-            terms(dest, q_rows, p)
+            sib_out[dest, p, rows, :] = sib[p]
+        for piece in range(PIECES) if rows == q_rows else (PIECES,):
+            sib_copy(dest, piece).start()
+        for p in range(PIECES):
+            own_part[dest, p, rows, :] = own[p]
 
     def each_dest(time, body):
         for way in range(2):
@@ -275,50 +302,58 @@
 
         run_copy(way, dest, piece).start()
 
-    def q_time(time, carry):
-        @pl.when(time < LAST - 1)
-        def _():
-            each_dest(time + 1, lambda way, dest: q_terms(dest))
-
+    def q_terms(time):
+        each_dest(time, lambda way, dest: terms(dest, q_rows))
+
+    def kv_terms(time):
+        each_dest(time, lambda way, dest: terms(dest, kv_rows))
+
+    def q_combine(time, p):
+        each_dest(time, lambda way, dest: combine(way, dest, p))
+
+    def kv_combine(time):
+        each_dest(time, lambda way, dest: combine(way, dest, PIECES))
+
+    def q_time(time):
+        q_terms(time)
         for p in range(PIECES):
-            each_dest(time, lambda way, dest: combine(way, dest, p))
-        return carry
-
-    each_dest(0, lambda way, dest: q_terms(dest))
-    lax.fori_loop(0, 2, q_time, 0)
+            q_combine(time, p)
+
+    q_time(0)
+    rest_of_attention()
+    q_time(1)
 
     for copy in dk_copies:
         copy.wait()
     pair_sum[...] = (
-        kv_part[pair]
-        + kv_in[0].astype(F32)
-        + kv_in[1].astype(F32)
-        + kv_in[2].astype(F32)
+        kv_part[pair] + kv_in[0].astype(F32) + kv_in[1].astype(F32) + kv_in[2].astype(F32)
     )
     z_out[...] = pair_sum[1 - z_hi].astype(BF16)
     dz_copy = remote(z_out, z_in, dkz.at[0], dkz.at[1], z_twin)
     dz_copy.start()
-    lax.fori_loop(2, 3, q_time, 0)
+    q_time(2)
+    q_terms(3)
+    q_combine(3, 0)
+    q_combine(3, 1)
     dz_copy.wait()
     back[128:160, :] = (pair_sum[z_hi] + z_in[...].astype(F32)).astype(BF16).reshape(32, tok_count)
-
-    def kv_terms(dest, carry):
-        terms(dest, kv_rows, PIECES)
-        return carry
-
-    lax.fori_loop(0, CHIPS, kv_terms, 0)
-
-    def kv_time(time, carry):
-        each_dest(time, lambda way, dest: combine(way, dest, PIECES))
-        return carry
-
-    def both(time, carry):
-        kv_time(time - 3, 0)
-        return q_time(time, carry)
-
-    lax.fori_loop(3, CHIPS - 1, both, 0)
-    q_terms(chip)
-    lax.fori_loop(2, CHIPS - 1, kv_time, 0)
+    kv_terms(0)
+    kv_terms(1)
+    kv_combine(0)
+    q_combine(3, 2)
+    kv_terms(2)
+    kv_combine(1)
+    q_terms(4)
+    q_combine(4, 0)
+    kv_terms(3)
+    kv_combine(2)
+    q_combine(4, 1)
+    kv_terms(4)
+    kv_combine(3)
+    terms(chip, q_rows)
+    q_combine(4, 2)
+    terms(chip, kv_rows)
+    kv_combine(4)
 
     for piece in range(PIECES + 1):
         rows = q_rows if piece < PIECES else kv_rows
@@ -372,9 +407,14 @@
             jax.ShapeDtypeStruct((6, 128, 128), F32),
             jax.ShapeDtypeStruct((6, 32, 128), F32),
         ),
-        in_specs=[pl.BlockSpec(memory_space=pl.ANY)] + [vmem] * 5,
+        in_specs=[pl.BlockSpec(memory_space=pltpu.HBM)] * 6,
         out_specs=(vmem, vmem, vmem),
         scratch_shapes=[
+            pltpu.VMEM((tok_count, 128), BF16),
+            pltpu.VMEM((6, 128, 128), BF16),
+            pltpu.VMEM((6, 128), BF16),
+            pltpu.VMEM((6, 32, 128), BF16),
+            pltpu.VMEM((6, 32), BF16),
             pltpu.VMEM((36, tok_count, STEP), BF16),
             pltpu.VMEM((12, 768, 128), BF16),
             pltpu.VMEM((12, 32, 768), BF16),
@@ -388,11 +428,16 @@
             pltpu.VMEM((2, 2, 16, tok_count), F32),
             pltpu.VMEM((2, 16, tok_count), BF16),
             pltpu.VMEM((2, 16, tok_count), BF16),
+            pltpu.VMEM((tok_count, length), F32),
+            pltpu.VMEM((tok_count, 128), BF16),
+            pltpu.VMEM((tok_count, length), BF16),
+            pltpu.VMEM((tok_count, length), BF16),
             pltpu.VMEM((CHIPS, PIECES, 160, STEP), BF16),
             pltpu.VMEM((CHIPS, PIECES, 160, STEP), BF16),
             pltpu.VMEM((CHIPS, PIECES, 160, STEP), BF16),
             pltpu.VMEM((CHIPS, PIECES, 160, STEP), BF16),
             pltpu.VMEM((2, CHIPS, PIECES, 160, STEP), BF16),
+            dma((5,)),
             dma(()),
             dma((12, PIECES + 1)),
             dma((3, CHIPS, PIECES + 1)),
@@ -408,7 +453,7 @@
             dma((3,)),
         ],
         compiler_params=pltpu.CompilerParams(
-            collective_id=0, has_side_effects=True, vmem_limit_bytes=48 * 1024 * 1024
+            collective_id=0, has_side_effects=True, vmem_limit_bytes=VLIM * 1024 * 1024
         ),
     )(
         tokens.reshape(tok_count, width),
@@ -416,7 +461,7 @@
         query_codes,
         query_scale,
         keyval_codes.transpose(0, 2, 1),
-        keyval_scale.T,
+        keyval_scale,
     )
     return out[0].reshape(context_gradient.shape), out[1], out[2].transpose(0, 2, 1)
 

time: 105 us -> 94.9 us (0.904)
  Pallas kernels: 97.3 us -> 87.8 us
  local copies, waits for them, and re-layouts: 6.13 us -> 4.87 us
    pallas_call x1, Pallas kernels: 97.3 us -> 87.8 us  [per_device(): pl.pallas_call(kernel, out_shape=(jax.ShapeDtypeStruct((tok_count, 128),...]
    unnamed x12 -> x3, local copies, waits for them, and re-layouts: 6.13 us -> 4.87 us
where the time goes in v2:
time: 94.9 us; the launch traced here: 93.3 us
  Pallas kernels  87.8 us (93%)
  local copies, waits for them, and re-layouts  4.87 us (5%)
    pallas_call x1, Pallas kernels, per_device(): pl.pallas_call(kernel, out_shape=(jax.ShapeDtypeStruct((tok_count, 128),...  87.8 us
    unnamed x3, local copies, waits for them, and re-layouts  4.87 us

profile of v2, /device:TPU:1, one launch (start us, length us, event | category | flops | bytes accessed | tf_op | source)
XLA Modules:
  0.0 93.3 jit_solution(11657730531338319980)
XLA Ops:
  0.6 87.8 %shard_map.85 = (bf16[512,128]{1,0:T(8,128)(2,1)}, f32[6,128,128]{2,1,0:T(8,128)}, f32[6,32,128]{2,1,0:T(8,128)}) custom-call(bf16[512,8192]{1,0:T(8,128)(2,1)} %bitcast.5, bf16[512,128]{1,0:T(8,128)(2,1)} %bitcast.6, bf16[6,128,128]{2,1,0:T(8,128)(2,1)} %qc_hbm.1, bf16[6,128]{1,0:T(8,128)(2,1)} %qs_hbm.1, bf16[6,32,128]{2,1,0:T(8,128)(2,1)} %bitcast.9, ...), custom_call_target="tpu_custom_call" | custom-call | tf_op jit(solution)/shard_map/pallas_call | solution.py:403
  88.4 1.6 %copy.12 = bf16[2,256,128]{2,1,0:T(8,128)(2,1)} copy(bf16[2,256,128]{2,1,0:T(8,128)(2,1)} %bitcast.7) | data formatting | bytes 262144
  90.0 1.8 %copy.13 = f32[6,128,128]{2,1,0:T(8,128)} copy(f32[6,128,128]{2,1,0:T(8,128)} %get-tuple-element.13) | data formatting | bytes 786432
  91.8 1.5 %copy.14 = f32[6,128,32]{1,2,0:T(8,128)} copy(f32[6,128,32]{1,2,0:T(8,128)} %bitcast.8) | data formatting | bytes 196608

commit v3 on v2

--- a/solution.py
+++ b/solution.py
@@ -17,6 +17,7 @@
 STEP = 256
 GROUP = 8
 VLIM = 60
+KV_LAG, Q_LAG, Z_SLOTS = 1, 3, 3
 
 
 def dot(a, b, dim_a=1, dim_b=0):
@@ -28,6 +29,8 @@
     ctx_ref, gq_ref, gkv_ref,
     grad_ref, qc_ref, qs_ref, kc_ref, ks_ref, x_all, wq, wkv, kv, q_acc, kv_acc, back, kv_part, kv_low, kv_in, pair_sum, z_out, z_in,
     grad_values, q_low, attend_low, scores_low, own_part, sib_out, sib_in, run_out, run_in,
+    kv_own, kv_sib_out, kv_sib_in, kv_run_out, kv_run_in, kv_total,
+    kv_s, kv_r,
     in_sem, x_sem, ag_r, ag_s, rs_r, rs_s, sib_r, sib_s, kvz, kvx_s, kvx_r, dkz, dkx_s, dkx_r,
 ):
     dp = lax.axis_index("dp")
@@ -69,16 +72,12 @@
         copy.start()
     loaded = x_all.at[pl.ds(0, 32)]
     x_copy = pltpu.make_async_copy(loaded, loaded, x_sem)
-    for i in range(32):
-        pltpu.make_async_copy(tok_hbm.at[:, pl.ds(i * STEP, STEP)], x_all.at[i], x_sem).start()
 
     barrier = pltpu.get_barrier_semaphore()
-    for to in (sibling, z_twin, x_mate(1), x_mate(2), x_mate(3)):
+    others = [(chip + i) % CHIPS for i in range(1, CHIPS)]
+    partners = [sibling, z_twin, x_mate(1), x_mate(2), x_mate(3)] + [{"dp": 2 * other + core} for other in others]
+    for to in partners:
         pl.semaphore_signal(barrier, inc=1, device_id=to, device_id_type=MESH)
-    for way in range(2):
-        @pl.when(place(way) < LAST)
-        def _():
-            pl.semaphore_signal(barrier, inc=1, device_id=ahead(way), device_id_type=MESH)
 
     for copy in small:
         copy.wait()
@@ -90,7 +89,7 @@
     for b in range(6):
         rows = pl.ds(b * 128, 128)
         wq[dp, rows, :] = (qc_ref[b].astype(F32) * qs_ref[b : b + 1, :].astype(F32)).astype(BF16)
-    pl.semaphore_wait(barrier, 7 - (chip == 0).astype(jnp.int32) - (chip == LAST).astype(jnp.int32))
+    pl.semaphore_wait(barrier, len(partners))
 
     def chunk(owner, piece):
         if isinstance(piece, int) and piece == 0:
@@ -148,60 +147,58 @@
             ag_send(src, piece, (way,))
         each_source(distance, body)
 
-    ag_send(chip, 0)
-    ag_send(chip, 1)
-    pass_on(1, 0)
-    ag_send(chip, 2)
-    pass_on(2, 0)
-    ag_send(chip, 3)
-    x_all[32:36] = jnp.zeros((4, tok_count, STEP), BF16)
-    x_copy.wait()
-    take(chip, 0)
-
-    def kv_step(d, carry):
-        pass_on(d, 0)
-        pass_on(1, d - 2)
-        each_source(d - 2, lambda way, src: take(src, 0))
-        return carry
-
-    lax.fori_loop(3, CHIPS, kv_step, 0)
-    pass_on(2, 1)
-    each_source(LAST - 1, lambda way, src: take(src, 0))
-    each_source(LAST, lambda way, src: take(src, 0))
-    kv[member] = kv_acc[...].astype(BF16).reshape(2, 16, tok_count)
+    order = [(0,0),(1,0),(2,0),(0,1),(3,0),(1,1),(0,2),(2,1),(3,1),(0,3),(1,2),(2,2),(0,4),(3,2),(1,3),(0,5),(2,3),(3,3)] + [(p, d) for d in (4, 5) for p in (1, 2, 3)]
+
+    def pass_slot(piece, distance):
+        if distance == 0:
+            ag_send(chip, piece)
+        else:
+            pass_on(distance, piece)
+
+    def use_slot(piece, distance):
+        if distance == 0:
+            take(chip, piece)
+        else:
+            each_source(distance, lambda way, src: take(src, piece))
+
+    pair = pl.ds(x_at * 2, 2)
     z_copy = remote(kv.at[member], kv.at[member], kvz.at[0], kvz.at[1], z_twin)
-    z_copy.start()
-    pass_on(2, 2)
-    pass_on(2, 3)
-    for p in range(PIECES):
-        take(chip, p + 1)
-
-    def q_step(d, carry):
-        for p in range(PIECES):
-            pass_on(d, p + 1)
-            each_source(d - 2, lambda way, src: take(src, p + 1))
-        return carry
-
-    lax.fori_loop(3, 4, q_step, 0)
-
-    pair = pl.ds(x_at * 2, 2)
-    z_copy.wait()
-    kv_copies = []
-    for delta in (1, 2, 3):
-        copy = remote(kv.at[pair], kv.at[pair], kvx_s.at[delta - 1], kvx_r.at[delta - 1], x_mate(delta))
-        copy.start()
-        kv_copies.append(copy)
-
-    lax.fori_loop(4, CHIPS, q_step, 0)
-    for p in range(PIECES):
-        each_source(LAST - 1, lambda way, src: take(src, p + 1))
+    kv_copies = [
+        remote(kv.at[pair], kv.at[pair], kvx_s.at[delta - 1], kvx_r.at[delta - 1], x_mate(delta))
+        for delta in (1, 2, 3)
+    ]
+    waiting = []
+    since_kv = None
+    for at, slot in enumerate(order):
+        pass_slot(*slot)
+        if at == 0:
+            for i in range(32):
+                pltpu.make_async_copy(tok_hbm.at[:, pl.ds(i * STEP, STEP)], x_all.at[i], x_sem).start()
+        if at == 3:
+            x_all[32:36] = jnp.zeros((4, tok_count, STEP), BF16)
+            x_copy.wait()
+        waiting.append((at + (KV_LAG if slot[0] == 0 else Q_LAG), slot))
+        if at >= 3:
+            for due, ready in [w for w in waiting if w[0] <= at]:
+                use_slot(*ready)
+                waiting.remove((due, ready))
+                if ready == (0, LAST):
+                    kv[member] = kv_acc[...].astype(BF16).reshape(2, 16, tok_count)
+                    z_copy.start()
+                    since_kv = at
+        if since_kv is not None and at == since_kv + Z_SLOTS:
+            z_copy.wait()
+            for copy in kv_copies:
+                copy.start()
+    last = waiting.pop()
+    for due, ready in waiting:
+        use_slot(*ready)
     for copy in kv_copies:
         copy.wait()
     for s in range(tok_count // length):
         at = slice(s * length, (s + 1) * length)
         grad_values[at, :] = dot(grad_ref[at, :], kv[:, 1, :, at].reshape(128, length))
-    for p in range(PIECES):
-        each_source(LAST, lambda way, src: take(src, p + 1))
+    use_slot(*last[1])
 
     factor = 1.0 / math.sqrt(128)
     keys = kv[:, 0].reshape(128, tok_count)
@@ -244,32 +241,30 @@
 
     def sib_copy(dest, piece):
         if piece < PIECES:
-            src, dst = sib_out.at[dest, piece, pl.ds(0, 128)], sib_in.at[dest, piece, pl.ds(0, 128)]
+            src, dst = sib_out.at[dest, piece], sib_in.at[dest, piece]
         else:
-            src, dst = sib_out.at[dest, :, pl.ds(128, 32)], sib_in.at[dest, :, pl.ds(128, 32)]
+            src, dst = kv_sib_out.at[dest], kv_sib_in.at[dest]
         return remote(src, dst, sib_s.at[dest, piece], sib_r.at[dest, piece], sibling)
 
-    def run_copy(way, dest, piece):
-        if piece < PIECES:
-            src, dst = run_out.at[dest, piece, pl.ds(0, 128)], run_in.at[way, dest, piece, pl.ds(0, 128)]
-        else:
-            src, dst = run_out.at[dest, :, pl.ds(128, 32)], run_in.at[way, dest, :, pl.ds(128, 32)]
-        return remote(src, dst, rs_s.at[dest, piece], rs_r.at[way, dest, piece], ahead(way))
+    def run_copy(way, dest, p):
+        src, dst = run_out.at[dest, p], run_in.at[way, dest, p]
+        return remote(src, dst, rs_s.at[dest, p], rs_r.at[way, dest, p], ahead(way))
 
     q_rows, kv_rows = slice(0, 128), slice(128, 160)
 
     def terms(dest, rows):
+        own_to, sib_to = (own_part, sib_out) if rows == q_rows else (kv_own, kv_sib_out)
         theirs = (2 * dest + 1 - core) * PIECES
         ours = (2 * dest + core) * PIECES
         low = back[rows, :]
         sib = [dot(low, x_all[theirs + p]).astype(BF16) for p in range(PIECES)]
         own = [dot(low, x_all[ours + p]).astype(BF16) for p in range(PIECES)]
         for p in range(PIECES):
-            sib_out[dest, p, rows, :] = sib[p]
+            sib_to[dest, p] = sib[p]
         for piece in range(PIECES) if rows == q_rows else (PIECES,):
             sib_copy(dest, piece).start()
         for p in range(PIECES):
-            own_part[dest, p, rows, :] = own[p]
+            own_to[dest, p] = own[p]
 
     def each_dest(time, body):
         for way in range(2):
@@ -278,41 +273,78 @@
             def _():
                 body(way, dest)
 
-    def combine(way, dest, piece):
-        rows = q_rows if piece < PIECES else kv_rows
-        pieces = (piece,) if piece < PIECES else range(PIECES)
-        sib_copy(dest, piece).wait_recv()
+    def combine(way, dest, p):
+        sib_copy(dest, p).wait_recv()
 
         @pl.when(place(way) > 0)
         def _():
-            run_copy(way, dest, piece).wait_recv()
-            for p in pieces:
-                run_out[dest, p, rows, :] = (
-                    own_part[dest, p, rows, :].astype(F32)
-                    + sib_in[dest, p, rows, :].astype(F32)
-                    + run_in[way, dest, p, rows, :].astype(F32)
-                ).astype(BF16)
+            run_copy(way, dest, p).wait_recv()
+            run_out[dest, p] = (
+                own_part[dest, p].astype(F32) + sib_in[dest, p].astype(F32) + run_in[way, dest, p].astype(F32)
+            ).astype(BF16)
 
         @pl.when(place(way) == 0)
         def _():
-            for p in pieces:
-                run_out[dest, p, rows, :] = (
-                    own_part[dest, p, rows, :].astype(F32) + sib_in[dest, p, rows, :].astype(F32)
-                ).astype(BF16)
-
-        run_copy(way, dest, piece).start()
+            run_out[dest, p] = (own_part[dest, p].astype(F32) + sib_in[dest, p].astype(F32)).astype(BF16)
+
+        run_copy(way, dest, p).start()
 
     def q_terms(time):
         each_dest(time, lambda way, dest: terms(dest, q_rows))
 
-    def kv_terms(time):
-        each_dest(time, lambda way, dest: terms(dest, kv_rows))
-
     def q_combine(time, p):
         each_dest(time, lambda way, dest: combine(way, dest, p))
 
-    def kv_combine(time):
-        each_dest(time, lambda way, dest: combine(way, dest, PIECES))
+    TURN = 2
+
+    def kv_copy(way, dest, straight):
+        slot = 2 * CHIPS + chip if straight else way * CHIPS + dest
+        to = {"dp": 2 * dest + core} if straight else ahead(way)
+        return remote(kv_run_out.at[dest], kv_run_in.at[slot], kv_s.at[dest], kv_r.at[slot], to)
+
+    def kv_arrived(slot):
+        part = kv_run_in.at[slot]
+        remote(part, part, kv_s.at[0], kv_r.at[slot], sibling).wait_recv()
+
+    def each_kv(time, body):
+        for way in range(2):
+            at = place(way)
+            base = at * (at <= TURN).astype(jnp.int32)
+            dest_at = LAST - time + base
+            @pl.when((time >= base) & (dest_at > at))
+            def _():
+                body(way, at, chip_of(way, dest_at))
+
+    def kv_terms(time):
+        each_kv(time, lambda way, at, dest: terms(dest, kv_rows))
+
+    def kv_send(time):
+        def body(way, at, dest):
+            sib_copy(dest, PIECES).wait_recv()
+            inner = (at > 0) & (at <= TURN)
+
+            @pl.when(inner)
+            def _():
+                kv_arrived(way * CHIPS + dest)
+                kv_run_out[dest] = (
+                    kv_own[dest].astype(F32)
+                    + kv_sib_in[dest].astype(F32)
+                    + kv_run_in[way * CHIPS + dest].astype(F32)
+                ).astype(BF16)
+
+            @pl.when(jnp.logical_not(inner))
+            def _():
+                kv_run_out[dest] = (kv_own[dest].astype(F32) + kv_sib_in[dest].astype(F32)).astype(BF16)
+
+            @pl.when(at < TURN)
+            def _():
+                kv_copy(way, dest, False).start()
+
+            @pl.when(at >= TURN)
+            def _():
+                kv_copy(way, dest, True).start()
+
+        each_kv(time, body)
 
     def q_time(time):
         q_terms(time)
@@ -339,44 +371,50 @@
     back[128:160, :] = (pair_sum[z_hi] + z_in[...].astype(F32)).astype(BF16).reshape(32, tok_count)
     kv_terms(0)
     kv_terms(1)
-    kv_combine(0)
+    kv_send(0)
     q_combine(3, 2)
     kv_terms(2)
-    kv_combine(1)
+    kv_send(1)
     q_terms(4)
     q_combine(4, 0)
     kv_terms(3)
-    kv_combine(2)
+    kv_send(2)
     q_combine(4, 1)
     kv_terms(4)
-    kv_combine(3)
+    kv_send(3)
     terms(chip, q_rows)
     q_combine(4, 2)
     terms(chip, kv_rows)
-    kv_combine(4)
-
-    for piece in range(PIECES + 1):
-        rows = q_rows if piece < PIECES else kv_rows
-        pieces = (piece,) if piece < PIECES else range(PIECES)
-        sib_copy(chip, piece).wait_recv()
-        for p in pieces:
-            run_sum = own_part[chip, p, rows, :].astype(F32) + sib_in[chip, p, rows, :].astype(F32)
-            if piece < PIECES:
-                gq_ref[2 * p : 2 * p + 2] = run_sum.T.reshape(2, 128, 128)
-            else:
-                gkv_ref[2 * p] = run_sum[:, 0:128]
-                gkv_ref[2 * p + 1] = run_sum[:, 128:256]
+    kv_send(4)
+
+    for p in range(PIECES):
+        sib_copy(chip, p).wait_recv()
+        gq_ref[2 * p : 2 * p + 2] = (
+            (own_part[chip, p].astype(F32) + sib_in[chip, p].astype(F32)).T.reshape(2, 128, 128)
+        )
         for way in range(2):
             @pl.when(place(way) > 0)
             def _():
-                run_copy(way, chip, piece).wait_recv()
-                for p in pieces:
-                    more = run_in[way, chip, p, rows, :].astype(F32)
-                    if piece < PIECES:
-                        gq_ref[2 * p : 2 * p + 2] += more.T.reshape(2, 128, 128)
-                    else:
-                        gkv_ref[2 * p] += more[:, 0:128]
-                        gkv_ref[2 * p + 1] += more[:, 128:256]
+                run_copy(way, chip, p).wait_recv()
+                gq_ref[2 * p : 2 * p + 2] += run_in[way, chip, p].astype(F32).T.reshape(2, 128, 128)
+    sib_copy(chip, PIECES).wait_recv()
+    kv_total[...] = kv_own[chip].astype(F32) + kv_sib_in[chip].astype(F32)
+    for way in range(2):
+        @pl.when((place(way) > 0) & (place(way) <= TURN))
+        def _():
+            kv_arrived(way * CHIPS + chip)
+            kv_total[...] += kv_run_in[way * CHIPS + chip].astype(F32)
+
+        for at in range(TURN, LAST):
+            @pl.when(place(way) > at)
+            def _():
+                kv_arrived(2 * CHIPS + chip_of(way, at))
+                kv_total[...] += kv_run_in[2 * CHIPS + chip_of(way, at)].astype(F32)
+    for b in range(6):
+        gkv_ref[b] = kv_total[b // 2, :, (b % 2) * 128 : (b % 2 + 1) * 128]
+
+    for other in others:
+        kv_copy(0, other, True).wait_send()
 
     def drain(at, carry):
         for piece in range(PIECES + 1):
@@ -385,9 +423,10 @@
                 def _():
                     ag_copy(at, piece, sibling, ag_s.at[way, at, piece]).wait_send()
 
-                @pl.when((at > chip) if way == 0 else (at < chip))
-                def _():
-                    run_copy(way, at, piece).wait_send()
+                if piece < PIECES:
+                    @pl.when((at > chip) if way == 0 else (at < chip))
+                    def _():
+                        run_copy(way, at, piece).wait_send()
             ag_copy(at, piece, sibling, ag_s.at[2, at, piece]).wait_send()
             sib_copy(at, piece).wait_send()
         return carry
@@ -432,17 +471,25 @@
             pltpu.VMEM((tok_count, 128), BF16),
             pltpu.VMEM((tok_count, length), BF16),
             pltpu.VMEM((tok_count, length), BF16),
-            pltpu.VMEM((CHIPS, PIECES, 160, STEP), BF16),
-            pltpu.VMEM((CHIPS, PIECES, 160, STEP), BF16),
-            pltpu.VMEM((CHIPS, PIECES, 160, STEP), BF16),
-            pltpu.VMEM((CHIPS, PIECES, 160, STEP), BF16),
-            pltpu.VMEM((2, CHIPS, PIECES, 160, STEP), BF16),
+            pltpu.VMEM((CHIPS, PIECES, 128, STEP), BF16),
+            pltpu.VMEM((CHIPS, PIECES, 128, STEP), BF16),
+            pltpu.VMEM((CHIPS, PIECES, 128, STEP), BF16),
+            pltpu.VMEM((CHIPS, PIECES, 128, STEP), BF16),
+            pltpu.VMEM((2, CHIPS, PIECES, 128, STEP), BF16),
+            pltpu.VMEM((CHIPS, PIECES, 32, STEP), BF16),
+            pltpu.VMEM((CHIPS, PIECES, 32, STEP), BF16),
+            pltpu.VMEM((CHIPS, PIECES, 32, STEP), BF16),
+            pltpu.VMEM((CHIPS, PIECES, 32, STEP), BF16),
+            pltpu.VMEM((3 * CHIPS, PIECES, 32, STEP), BF16),
+            pltpu.VMEM((PIECES, 32, STEP), F32),
+            dma((CHIPS,)),
+            dma((3 * CHIPS,)),
             dma((5,)),
             dma(()),
             dma((12, PIECES + 1)),
             dma((3, CHIPS, PIECES + 1)),
-            dma((2, CHIPS, PIECES + 1)),
-            dma((CHIPS, PIECES + 1)),
+            dma((2, CHIPS, PIECES)),
+            dma((CHIPS, PIECES)),
             dma((CHIPS, PIECES + 1)),
             dma((CHIPS, PIECES + 1)),
             dma((2,)),

time: 94.9 us -> 90.9 us (0.958); the launches traced: 93.3 us -> 90.7 us
  Pallas kernels: 87.8 us -> 85.2 us
    pallas_call x1, Pallas kernels: 87.8 us -> 85.2 us  [per_device(): pl.pallas_call(kernel, out_shape=(jax.ShapeDtypeStruct((tok_count, 128),...]
where the time goes in v3:
time: 90.9 us; the launch traced here: 90.7 us
  Pallas kernels  85.2 us (94%)
  local copies, waits for them, and re-layouts  4.87 us (5%)
    pallas_call x1, Pallas kernels, per_device(): pl.pallas_call(kernel, out_shape=(jax.ShapeDtypeStruct((tok_count, 128),...  85.2 us
    unnamed x3, local copies, waits for them, and re-layouts  4.87 us

profile of v3, /device:TPU:1, one launch (start us, length us, event | category | flops | bytes accessed | tf_op | source)
XLA Modules:
  0.0 90.7 jit_solution(4905858262378130780)
XLA Ops:
  0.6 85.2 %shard_map.85 = (bf16[512,128]{1,0:T(8,128)(2,1)}, f32[6,128,128]{2,1,0:T(8,128)}, f32[6,32,128]{2,1,0:T(8,128)}) custom-call(bf16[512,8192]{1,0:T(8,128)(2,1)} %bitcast.5, bf16[512,128]{1,0:T(8,128)(2,1)} %bitcast.6, bf16[6,128,128]{2,1,0:T(8,128)(2,1)} %qc_hbm.1, bf16[6,128]{1,0:T(8,128)(2,1)} %qs_hbm.1, bf16[6,32,128]{2,1,0:T(8,128)(2,1)} %bitcast.9, ...), custom_call_target="tpu_custom_call" | custom-call | tf_op jit(solution)/shard_map/pallas_call | solution.py:442
  85.8 1.6 %copy.12 = bf16[2,256,128]{2,1,0:T(8,128)(2,1)} copy(bf16[2,256,128]{2,1,0:T(8,128)(2,1)} %bitcast.7) | data formatting | bytes 262144
  87.4 1.8 %copy.13 = f32[6,128,128]{2,1,0:T(8,128)} copy(f32[6,128,128]{2,1,0:T(8,128)} %get-tuple-element.13) | data formatting | bytes 786432
  89.2 1.5 %copy.14 = f32[6,128,32]{1,2,0:T(8,128)} copy(f32[6,128,32]{1,2,0:T(8,128)} %bitcast.8) | data formatting | bytes 196608

commit v4 on v3

--- a/solution.py
+++ b/solution.py
@@ -295,7 +295,7 @@
     def q_combine(time, p):
         each_dest(time, lambda way, dest: combine(way, dest, p))
 
-    TURN = 2
+    TURN = 1
 
     def kv_copy(way, dest, straight):
         slot = 2 * CHIPS + chip if straight else way * CHIPS + dest
@@ -351,7 +351,16 @@
         for p in range(PIECES):
             q_combine(time, p)
 
-    q_time(0)
+    def first_terms(way, dest):
+        for p in range(PIECES):
+            sib_out[dest, p] = dot(back[q_rows, :], x_all[(2 * dest + 1 - core) * PIECES + p]).astype(BF16)
+            sib_copy(dest, p).start()
+        for p in range(PIECES):
+            own_part[dest, p] = dot(back[q_rows, :], x_all[(2 * dest + core) * PIECES + p]).astype(BF16)
+
+    each_dest(0, first_terms)
+    for p in range(PIECES):
+        q_combine(0, p)
     rest_of_attention()
     q_time(1)
 
@@ -387,6 +396,19 @@
     terms(chip, kv_rows)
     kv_send(4)
 
+    def drain(at, carry):
+        for way in range(2):
+            @pl.when((place(way) < LAST) & ((at <= chip) if way == 0 else (at >= chip)))
+            def _():
+                for piece in range(PIECES + 1):
+                    ag_copy(at, piece, sibling, ag_s.at[way, at, piece]).wait_send()
+        for piece in range(PIECES + 1):
+            ag_copy(at, piece, sibling, ag_s.at[2, at, piece]).wait_send()
+            sib_copy(at, piece).wait_send()
+        return carry
+
+    lax.fori_loop(0, CHIPS, drain, 0)
+
     for p in range(PIECES):
         sib_copy(chip, p).wait_recv()
         gq_ref[2 * p : 2 * p + 2] = (
@@ -416,22 +438,15 @@
     for other in others:
         kv_copy(0, other, True).wait_send()
 
-    def drain(at, carry):
-        for piece in range(PIECES + 1):
-            for way in range(2):
-                @pl.when((place(way) < LAST) & ((at <= chip) if way == 0 else (at >= chip)))
-                def _():
-                    ag_copy(at, piece, sibling, ag_s.at[way, at, piece]).wait_send()
-
-                if piece < PIECES:
-                    @pl.when((at > chip) if way == 0 else (at < chip))
-                    def _():
-                        run_copy(way, at, piece).wait_send()
-            ag_copy(at, piece, sibling, ag_s.at[2, at, piece]).wait_send()
-            sib_copy(at, piece).wait_send()
+    def drain_sums(at, carry):
+        for way in range(2):
+            @pl.when((at > chip) if way == 0 else (at < chip))
+            def _():
+                for p in range(PIECES):
+                    run_copy(way, at, p).wait_send()
         return carry
 
-    lax.fori_loop(0, CHIPS, drain, 0)
+    lax.fori_loop(0, CHIPS, drain_sums, 0)
 
 
 def per_device(tokens, context_gradient, query_codes, query_scale, keyval_codes, keyval_scale):

time: 90.9 us -> 90.1 us (level)
  no operation moved by 1% of the time
where the time goes in v4:
time: 90.1 us; the launch traced here: 89.8 us
  Pallas kernels  84.3 us (94%)
  local copies, waits for them, and re-layouts  4.87 us (5%)
    pallas_call x1, Pallas kernels, per_device(): pl.pallas_call(kernel, out_shape=(jax.ShapeDtypeStruct((tok_count, 128),...  84.3 us
    unnamed x3, local copies, waits for them, and re-layouts  4.87 us

profile of v4, /device:TPU:1, one launch (start us, length us, event | category | flops | bytes accessed | tf_op | source)
XLA Modules:
  0.0 89.8 jit_solution(10727543267048378077)
XLA Ops:
  0.6 84.3 %shard_map.85 = (bf16[512,128]{1,0:T(8,128)(2,1)}, f32[6,128,128]{2,1,0:T(8,128)}, f32[6,32,128]{2,1,0:T(8,128)}) custom-call(bf16[512,8192]{1,0:T(8,128)(2,1)} %bitcast.5, bf16[512,128]{1,0:T(8,128)(2,1)} %bitcast.6, bf16[6,128,128]{2,1,0:T(8,128)(2,1)} %qc_hbm.1, bf16[6,128]{1,0:T(8,128)(2,1)} %qs_hbm.1, bf16[6,32,128]{2,1,0:T(8,128)(2,1)} %bitcast.9, ...), custom_call_target="tpu_custom_call" | custom-call | tf_op jit(solution)/shard_map/pallas_call | solution.py:457
  84.9 1.6 %copy.12 = bf16[2,256,128]{2,1,0:T(8,128)(2,1)} copy(bf16[2,256,128]{2,1,0:T(8,128)(2,1)} %bitcast.7) | data formatting | bytes 262144
  86.5 1.8 %copy.13 = f32[6,128,128]{2,1,0:T(8,128)} copy(f32[6,128,128]{2,1,0:T(8,128)} %get-tuple-element.13) | data formatting | bytes 786432
  88.3 1.5 %copy.14 = f32[6,128,32]{1,2,0:T(8,128)} copy(f32[6,128,32]{1,2,0:T(8,128)} %bitcast.8) | data formatting | bytes 196608
